TPU v7x, 128 devices: a whole 4x4x4 slice. The times are simulated.
128 devices in a mesh: ctx: 32 (over y, z, core), uly: 4 (over x).
Axes of the slice: x: 4, y: 4, z: 4, core: 2. Of those that a mesh axis runs over, the one named last changes fastest.
Arguments:
- queries: bfloat16 [24576, 4096], P(('ctx', 'uly')), may hold values from -24 to 24
- keys: bfloat16 [24576, 4096], P(('ctx', 'uly')), may hold values from -6 to 6
- values: bfloat16 [24576, 4096], P(('ctx', 'uly')), may hold values from -6 to 6
- d_out: bfloat16 [24576, 4096], P(('ctx', 'uly')), may hold values from -6 to 6
- doc_lengths: int32 [64], replicated, may hold values from 1 to 768, 24576 in all
Outputs:
- attn_out: bfloat16 [24576, 4096], P(('ctx', 'uly'))
- d_queries: bfloat16 [24576, 4096], P(('ctx', 'uly'))
- d_keys: bfloat16 [24576, 4096], P(('ctx', 'uly'))
- d_values: bfloat16 [24576, 4096], P(('ctx', 'uly'))
Inputs may be any that keep to these rules, and one draw needn't show every extreme that they name: `doc_lengths`: the lengths sum to 24576.
All inputs are finite; a program needn't handle non-finite values.
Results may differ from a plain program's by a relative error of at most 0.012.
The roundings to bfloat16 on the way count: a program that leaves them out, or rounds other values in their place, can miss the bound.
Values may be sent and summed in bfloat16 or wider, within the bound.
No kernel may reach another device: no remote copies, remote signals or barrier semaphores. Data moves between devices by JAX's collectives and lax.ppermute only.
A program may use at most 192 MiB of HBM per device.

v0:
```python
import jax
import jax.numpy as jnp
from jax import lax
from jax.sharding import PartitionSpec as P

HEAD_DIM = 128
masked_score = -1e30


def shifted(value, axis, by):
    count = lax.axis_size(axis)
    pairs = [(i, i + by) for i in range(count) if 0 <= i + by < count]
    return lax.ppermute(value, axis, pairs)


def doc_index(positions, doc_ends):
    inside = jnp.sum((doc_ends[None, :] <= positions[:, None]).astype(jnp.int32), axis=1)
    return jnp.where(positions < 0, -1, inside)


def contract_last(left, right):
    return lax.dot_general(
        left, right, (((1,), (1,)), ((), ())), preferred_element_type=jnp.float32
    )


def contract_first(left, right):
    return lax.dot_general(
        left, right, (((0,), (0,)), ((), ())), preferred_element_type=jnp.float32
    )


def head_slice(array, column):
    return lax.dynamic_slice_in_dim(array, column, HEAD_DIM, 1)


def on_device(queries, keys, values, d_out, doc_lengths):
    query_loc, key_loc, value_loc, grad_loc = (
        lax.all_to_all(queries, "uly", split_axis=1, concat_axis=0, tiled=True),
        lax.all_to_all(keys, "uly", split_axis=1, concat_axis=0, tiled=True),
        lax.all_to_all(values, "uly", split_axis=1, concat_axis=0, tiled=True),
        lax.all_to_all(d_out, "uly", split_axis=1, concat_axis=0, tiled=True),
    )
    row_count = query_loc.shape[0]
    columns = query_loc.shape[1]
    heads_here = columns // HEAD_DIM
    score_scale = HEAD_DIM ** (-0.5)
    doc_iota = jnp.arange(doc_lengths.shape[0], dtype=jnp.int32)
    doc_ends = jnp.sum(
        jnp.where(doc_iota[None, :] <= doc_iota[:, None], doc_lengths[None, :], 0), axis=1
    )
    shard_index = lax.axis_index("ctx")
    offsets = []
    offsets = offsets + [1, -1]
    row_iota = jnp.arange(row_count, dtype=jnp.int32)
    own_docs = doc_index(shard_index * row_count + row_iota, doc_ends)
    key_list = [key_loc]
    value_list = [value_loc]
    doc_list = [own_docs]
    for offset in offsets:
        moved_keys, moved_values = shifted((key_loc, value_loc), "ctx", offset)
        key_list.append(moved_keys)
        value_list.append(moved_values)
        doc_list.append(doc_index((shard_index - offset) * row_count + row_iota, doc_ends))
    key_all = jnp.concatenate(key_list, axis=0)
    value_all = jnp.concatenate(value_list, axis=0)
    near_docs = jnp.concatenate(doc_list, axis=0)
    query_same = own_docs[:, None] == near_docs[None, :]
    near_rows = key_all.shape[0]
    part_shape = (near_rows, columns)

    def query_step(head_index, carry):
        out_acc, dq_acc, stat_total, stat_delta, dk_acc, dv_acc = carry
        column = head_index * HEAD_DIM
        query_head = head_slice(query_loc, column)
        key_head = head_slice(key_all, column)
        value_head = head_slice(value_all, column)
        grad_head = head_slice(grad_loc, column)
        scores = jnp.where(
            query_same, score_scale * contract_last(query_head, key_head), masked_score
        )
        row_max = jnp.max(scores, axis=1, keepdims=True)
        log_total = row_max + jnp.log(jnp.sum(jnp.exp(scores - row_max), axis=1, keepdims=True))
        weights = jnp.exp(scores - log_total).astype(jnp.bfloat16)
        out_head = jnp.dot(weights, value_head, preferred_element_type=jnp.float32).astype(
            jnp.bfloat16
        )
        row_delta = jnp.sum(
            grad_head.astype(jnp.float32) * lax.optimization_barrier(out_head).astype(jnp.float32),
            axis=1,
            keepdims=True,
        )
        grad_scores = (
            lax.optimization_barrier(weights).astype(jnp.float32)
            * (contract_last(grad_head, value_head) - row_delta)
        ).astype(jnp.bfloat16)
        dq_head = (
            score_scale * jnp.dot(grad_scores, key_head, preferred_element_type=jnp.float32)
        ).astype(jnp.bfloat16)
        out_acc = lax.dynamic_update_slice_in_dim(out_acc, out_head, column, 1)
        dq_acc = lax.dynamic_update_slice_in_dim(dq_acc, dq_head, column, 1)
        stat_total = lax.dynamic_update_slice_in_dim(stat_total, log_total, head_index, 1)
        stat_delta = lax.dynamic_update_slice_in_dim(stat_delta, row_delta, head_index, 1)
        dk_acc = lax.dynamic_update_slice_in_dim(
            dk_acc, score_scale * contract_first(grad_scores, query_head), column, 1
        )
        dv_acc = lax.dynamic_update_slice_in_dim(
            dv_acc, contract_first(weights, grad_head), column, 1
        )
        return (out_acc, dq_acc, stat_total, stat_delta, dk_acc, dv_acc)

    start_carry = (
        jnp.zeros((row_count, columns), jnp.bfloat16),
        jnp.zeros((row_count, columns), jnp.bfloat16),
        jnp.zeros((row_count, heads_here), jnp.float32),
        jnp.zeros((row_count, heads_here), jnp.float32),
        jnp.zeros(part_shape, jnp.float32),
        jnp.zeros(part_shape, jnp.float32),
    )
    out_loc, dq_loc, stat_total, stat_delta, dk_acc, dv_acc = lax.fori_loop(
        0, heads_here, query_step, start_carry
    )
    key_sum = dk_acc[:row_count]
    value_sum = dv_acc[:row_count]
    for segment, offset in enumerate(offsets):
        first_row = (segment + 1) * row_count
        back_keys, back_values = shifted(
            (dk_acc[first_row : first_row + row_count], dv_acc[first_row : first_row + row_count]),
            "ctx",
            -offset,
        )
        key_sum = key_sum + back_keys
        value_sum = value_sum + back_values
    dk_loc = key_sum.astype(jnp.bfloat16)
    dv_loc = value_sum.astype(jnp.bfloat16)
    attn_out, d_queries, d_keys, d_values = (
        lax.all_to_all(out_loc, "uly", split_axis=0, concat_axis=1, tiled=True),
        lax.all_to_all(dq_loc, "uly", split_axis=0, concat_axis=1, tiled=True),
        lax.all_to_all(dk_loc, "uly", split_axis=0, concat_axis=1, tiled=True),
        lax.all_to_all(dv_loc, "uly", split_axis=0, concat_axis=1, tiled=True),
    )
    return (attn_out, d_queries, d_keys, d_values)


def solution(mesh):
    return jax.shard_map(
        on_device,
        mesh=mesh,
        in_specs=(
            P(("ctx", "uly"), None),
            P(("ctx", "uly"), None),
            P(("ctx", "uly"), None),
            P(("ctx", "uly"), None),
            P(),
        ),
        out_specs=(
            P(("ctx", "uly"), None),
            P(("ctx", "uly"), None),
            P(("ctx", "uly"), None),
            P(("ctx", "uly"), None),
        ),
        check_vma=False,
    )
```

profile of v0, /device:TPU:88, one launch (start us, length us, event | category | flops | bytes accessed | tf_op | source)
XLA Modules:
  0.0 372.4 jit_solution(8924392566214620014)
XLA Ops:
  0.6 2.8 copy.50
  3.5 4.3 %all-to-all-start.2 = ((bf16[192,4,1024]{2,0,1:T(8,128)(2,1)}), bf16[192,4,1024]{2,0,1:T(8,128)(2,1)S(1)}, u32[]{:S(2)}, u32[]{:S(2)}) async-start(bf16[192,4,1024]{2,0,1:T(8,128)(2,1)} %bitcast.45), calls=%async_computation.2 | async-start | bytes 3145728 | tf_op jit(solution)/shard_map/all_to_all | solution.py:41
  9.1 19.4 %all-to-all-done.2 = bf16[192,4,1024]{2,0,1:T(8,128)(2,1)S(1)} async-done(((bf16[192,4,1024]{2,0,1:T(8,128)(2,1)}), bf16[192,4,1024]{2,0,1:T(8,128)(2,1)S(1)}, u32[]{:S(2)}, u32[]{:S(2)}) %all-to-all-start.2) | async-done | bytes 1572896 | tf_op jit(solution)/shard_map/all_to_all | solution.py:41
  28.5 4.3 %all-to-all-start.1 = ((bf16[192,4,1024]{2,0,1:T(8,128)(2,1)}), bf16[192,4,1024]{2,0,1:T(8,128)(2,1)}, u32[]{:S(2)}, u32[]{:S(2)}) async-start(bf16[192,4,1024]{2,0,1:T(8,128)(2,1)} %bitcast.46), calls=%async_computation.1 | async-start | bytes 3145728 | tf_op jit(solution)/shard_map/all_to_all | solution.py:40
  34.7 2.4 collective-permute-start.2
  38.5 14.2 %all-to-all-done.1 = bf16[192,4,1024]{2,0,1:T(8,128)(2,1)} async-done(((bf16[192,4,1024]{2,0,1:T(8,128)(2,1)}), bf16[192,4,1024]{2,0,1:T(8,128)(2,1)}, u32[]{:S(2)}, u32[]{:S(2)}) %all-to-all-start.1) | async-done | bytes 1572896 | tf_op jit(solution)/shard_map/all_to_all | solution.py:40
  52.7 3.6 all-to-all-start
  56.3 2.7 copy.49
  60.9 2.4 collective-permute-start
  63.6 11.5 %all-to-all-done = bf16[192,4,1024]{2,0,1:T(8,128)(2,1)S(1)} async-done(((bf16[192,4,1024]{2,0,1:T(8,128)(2,1)}), bf16[192,4,1024]{2,0,1:T(8,128)(2,1)S(1)}, u32[]{:S(2)}, u32[]{:S(2)}) %all-to-all-start) | async-done | bytes 1572896 | tf_op jit(solution)/shard_map/all_to_all | solution.py:39
  76.2 3.6 all-to-all-start.3
  79.9 3.8 %pad_maximum_fusion.1 = bf16[2304,1024]{1,0:T(8,128)(2,1)} fusion(bf16[768,1024]{1,0:T(8,128)(2,1)} %collective-permute-done.3, bf16[768,1024]{1,0:T(8,128)(2,1)} %collective-permute-done.2, bf16[768,1024]{1,0:T(8,128)(2,1)S(1)} %bitcast.59), kind=kLoop, calls=%fused_computation.30 | loop fusion | flops 14155776 | bytes 9437184 | tf_op jit(solution)/shard_map/concatenate | solution.py:66
  83.7 4.0 %pad_maximum_fusion = bf16[2304,1024]{1,0:T(8,128)(2,1)} fusion(bf16[768,1024]{1,0:T(8,128)(2,1)} %collective-permute-done.1, bf16[768,1024]{1,0:T(8,128)(2,1)} %collective-permute-done, bf16[768,1024]{1,0:T(8,128)(2,1)} %bitcast.3), kind=kLoop, calls=%fused_computation.29 | loop fusion | flops 14155776 | bytes 9437184 | tf_op jit(solution)/shard_map/concatenate | solution.py:65
  87.7 10.1 %all-to-all-done.3 = bf16[192,4,1024]{2,0,1:T(8,128)(2,1)S(1)} async-done(((bf16[192,4,1024]{2,0,1:T(8,128)(2,1)}), bf16[192,4,1024]{2,0,1:T(8,128)(2,1)S(1)}, u32[]{:S(2)}, u32[]{:S(2)}) %all-to-all-start.3) | async-done | bytes 1572896 | tf_op jit(solution)/shard_map/all_to_all | solution.py:42
  99.3 4.8 %broadcast.59.clone = f32[2304,1024]{1,0:T(8,128)} broadcast(f32[]{:T(128)} %constant.69.clone.1), dimensions={} | broadcast | bytes 9437188 | tf_op jit(solution)/shard_map/broadcast.9
  104.1 4.8 %broadcast.59 = f32[2304,1024]{1,0:T(8,128)} broadcast(f32[]{:T(128)} %constant.69.clone.1), dimensions={} | broadcast | bytes 9437188 | tf_op jit(solution)/shard_map/broadcast.9
  109.0 141.8 %while.20 = (s32[]{:T(128)}, bf16[768,1024]{1,0:T(8,128)(2,1)}, bf16[768,1024]{1,0:T(8,128)(2,1)S(1)}, f32[2304,1024]{1,0:T(8,128)}, f32[2304,1024]{1,0:T(8,128)...) while((s32[]{:T(128)}, bf16[768,1024]{1,0:T(8,128)(2,1)}, ...), condition=%wide.region_8.9_spmd.clone, body=%wide.region_4.8_spmd.clone.sunk | while | flops 2740124160 | bytes 52541632 | solution.py:120
  109.0 2.6 fusion.47
  113.9 2.8 constant_dynamic-update-slice_fusion.2
  119.1 2.2 fusion.48
  121.3 3.2 fusion.49
  126.7 2.6 fusion.47
  131.6 2.8 constant_dynamic-update-slice_fusion.2
  139.0 3.2 fusion.49
  144.4 2.6 fusion.47
  149.3 2.8 constant_dynamic-update-slice_fusion.2
  154.5 2.2 fusion.48
  156.7 3.2 fusion.49
  162.1 2.6 fusion.47
  167.0 2.8 constant_dynamic-update-slice_fusion.2
  172.2 2.2 fusion.48
  174.4 3.2 fusion.49
  177.6 2.2 convolution_dynamic-update-slice_fusion.2
  179.9 2.6 fusion.47
  184.8 2.8 constant_dynamic-update-slice_fusion.2
  192.2 3.2 fusion.49
  195.4 2.2 convolution_dynamic-update-slice_fusion.2
  197.7 2.6 fusion.47
  202.6 2.8 constant_dynamic-update-slice_fusion.2
  210.0 3.2 fusion.49
  215.3 2.6 fusion.47
  220.2 2.8 constant_dynamic-update-slice_fusion.2
  227.7 3.1 fusion.49
  233.0 2.6 fusion.47
  238.0 2.8 constant_dynamic-update-slice_fusion.2
  243.2 2.2 fusion.48
  245.4 3.1 fusion.49
  250.7 6.7 %fusion.20 = (f32[768,1024]{1,0:T(8,128)}, f32[768,1024]{1,0:T(8,128)}) fusion(f32[2304,1024]{1,0:T(8,128)} %get-tuple-element.179), kind=kLoop, calls=%fused_computation.50 | loop fusion | bytes 12582912 | tf_op jit(solution)/shard_map/slice | solution.py:128
  259.4 2.4 collective-permute-start.7
  261.8 3.3 fusion.21
  265.1 3.1 collective-permute-start.4
  270.4 23.3 %all_to_all.152 = bf16[4,192,1024]{2,1,0:T(8,128)(2,1)S(1)} all-to-all(bf16[4,192,1024]{2,1,0:T(8,128)(2,1)S(1)} %bitcast.63), channel_id=1, replica_groups=mesh['ctx'=32,'uly'=4] {'uly'}, dimensions={0} | all-to-all | bytes 3145728 | tf_op jit(solution)/shard_map/all_to_all | solution.py:138
  293.6 3.6 all-to-all-start.4
  298.3 5.8 %add_convert_fusion = bf16[768,1024]{1,0:T(8,128)(2,1)} fusion(f32[768,1024]{1,0:T(8,128)} %collective-permute-done.7, f32[768,1024]{1,0:T(8,128)} %collective-permute-done.6, f32[2304,1024]{1,0:T(8,128)} %get-tuple-element.179), kind=kLoop, calls=%fused_computation.31 | loop fusion | flops 2359296 | bytes 11010048 | tf_op jit(solution)/shard_map/convert_element_type | solution.py:135
  304.1 15.1 %all-to-all-done.4 = bf16[4,192,1024]{2,1,0:T(8,128)(2,1)S(1)} async-done(((bf16[4,192,1024]{2,1,0:T(8,128)(2,1)}), bf16[4,192,1024]{2,1,0:T(8,128)(2,1)S(1)}, u32[]{:S(2)}, u32[]{:S(2)}) %all-to-all-start.4) | async-done | bytes 1572896 | tf_op jit(solution)/shard_map/all_to_all | solution.py:137
  319.2 4.3 %all-to-all-start.7 = ((bf16[4,192,1024]{2,1,0:T(8,128)(2,1)}), bf16[4,192,1024]{2,1,0:T(8,128)(2,1)}, u32[]{:S(2)}, u32[]{:S(2)}) async-start(bf16[4,192,1024]{2,1,0:T(8,128)(2,1)} %bitcast.65), calls=%async_computation.7 | async-start | bytes 3145728 | tf_op jit(solution)/shard_map/all_to_all | solution.py:140
  323.5 4.7 %collective-permute-done.4 = f32[768,1024]{1,0:T(8,128)} collective-permute-done((f32[768,1024]{1,0:T(8,128)}, f32[768,1024]{1,0:T(8,128)}, u32[]{:S(2)}, u32[]{:S(2)}) %collective-permute-start.4) | collective-permute-done | bytes 3145760 | tf_op jit(solution)/shard_map/ppermute | solution.py:13
  328.2 3.8 %collective-permute-done.5 = f32[768,1024]{1,0:T(8,128)} collective-permute-done((f32[768,1024]{1,0:T(8,128)}, f32[768,1024]{1,0:T(8,128)}, u32[]{:S(2)}, u32[]{:S(2)}) %collective-permute-start.5) | collective-permute-done | bytes 3145760 | tf_op jit(solution)/shard_map/ppermute | solution.py:13
  332.0 5.8 %add_convert_fusion.1 = bf16[768,1024]{1,0:T(8,128)(2,1)} fusion(f32[768,1024]{1,0:T(8,128)} %collective-permute-done.5, f32[768,1024]{1,0:T(8,128)} %collective-permute-done.4, f32[2304,1024]{1,0:T(8,128)} %get-tuple-element.178), kind=kLoop, calls=%fused_computation.32 | loop fusion | flops 2359296 | bytes 11010048 | tf_op jit(solution)/shard_map/convert_element_type | solution.py:134
  337.8 7.0 %all-to-all-done.7 = bf16[4,192,1024]{2,1,0:T(8,128)(2,1)} async-done(((bf16[4,192,1024]{2,1,0:T(8,128)(2,1)}), bf16[4,192,1024]{2,1,0:T(8,128)(2,1)}, u32[]{:S(2)}, u32[]{:S(2)}) %all-to-all-start.7) | async-done | bytes 1572896 | tf_op jit(solution)/shard_map/all_to_all | solution.py:140
  344.9 4.3 %all-to-all-start.6 = ((bf16[4,192,1024]{2,1,0:T(8,128)(2,1)}), bf16[4,192,1024]{2,1,0:T(8,128)(2,1)}, u32[]{:S(2)}, u32[]{:S(2)}) async-start(bf16[4,192,1024]{2,1,0:T(8,128)(2,1)} %bitcast.66), calls=%async_computation.6 | async-start | bytes 3145728 | tf_op jit(solution)/shard_map/all_to_all | solution.py:139
  351.8 2.7 copy.44
  354.5 15.2 %all-to-all-done.6 = bf16[4,192,1024]{2,1,0:T(8,128)(2,1)} async-done(((bf16[4,192,1024]{2,1,0:T(8,128)(2,1)}), bf16[4,192,1024]{2,1,0:T(8,128)(2,1)}, u32[]{:S(2)}, u32[]{:S(2)}) %all-to-all-start.6) | async-done | bytes 1572896 | tf_op jit(solution)/shard_map/all_to_all | solution.py:139
  369.7 2.7 copy.43
  (84 shorter events, 76.5 us)
Async XLA Ops:
  0.6 7.1 %copy-start.2 = (bf16[192,4096]{1,0:T(8,128)(2,1)S(1)}, bf16[192,4096]{1,0:T(8,128)(2,1)}, u32[]{:S(2)}) copy-start(bf16[192,4096]{1,0:T(8,128)(2,1)} %param.8) | copy-start | bytes 4718596
  3.5 25.0 %all-to-all-start.2 = ((bf16[192,4,1024]{2,0,1:T(8,128)(2,1)}), bf16[192,4,1024]{2,0,1:T(8,128)(2,1)S(1)}, u32[]{:S(2)}, u32[]{:S(2)}) async-start(bf16[192,4,1024]{2,0,1:T(8,128)(2,1)} %bitcast.45), calls=%async_computation.2 | async-start | bytes 3145728 | tf_op jit(solution)/shard_map/all_to_all | solution.py:41
  9.1 28.1 %copy-start.3 = (bf16[192,4096]{1,0:T(8,128)(2,1)S(1)}, bf16[192,4096]{1,0:T(8,128)(2,1)}, u32[]{:S(2)}) copy-start(bf16[192,4096]{1,0:T(8,128)(2,1)} %param.7) | copy-start | bytes 4718596
  28.5 24.2 %all-to-all-start.1 = ((bf16[192,4,1024]{2,0,1:T(8,128)(2,1)}), bf16[192,4,1024]{2,0,1:T(8,128)(2,1)}, u32[]{:S(2)}, u32[]{:S(2)}) async-start(bf16[192,4,1024]{2,0,1:T(8,128)(2,1)} %bitcast.46), calls=%async_computation.1 | async-start | bytes 3145728 | tf_op jit(solution)/shard_map/all_to_all | solution.py:40
  32.8 47.0 %collective-permute-start.3 = (bf16[768,1024]{1,0:T(8,128)(2,1)S(1)}, bf16[768,1024]{1,0:T(8,128)(2,1)}, u32[]{:S(2)}, u32[]{:S(2)}) collective-permute-start(bf16[768,1024]{1,0:T(8,128)(2,1)S(1)} %bitcast.57), channel_id=1, source_target_pairs={{4,0},{8,4},{12,8},{16,12},{20,16},{24,20},{28,24},{32,28},{36,32}... | collective-permute-start | bytes 4718600 | tf_op jit(solution)/shard_map/ppermute | solution.py:13
  34.7 45.1 %collective-permute-start.2 = (bf16[768,1024]{1,0:T(8,128)(2,1)S(1)}, bf16[768,1024]{1,0:T(8,128)(2,1)}, u32[]{:S(2)}, u32[]{:S(2)}) collective-permute-start(bf16[768,1024]{1,0:T(8,128)(2,1)S(1)} %bitcast.58), channel_id=1, source_target_pairs={{0,4},{4,8},{8,12},{12,16},{16,20},{20,24},{24,28},{28,32},{32,36}... | collective-permute-start | bytes 4718600 | tf_op jit(solution)/shard_map/ppermute | solution.py:13
  38.5 24.9 %copy-start.4 = (s32[64]{0:T(128)S(1)}, s32[64]{0:T(128)}, u32[]{:S(2)}) copy-start(s32[64]{0:T(128)} %param.11) | copy-start | bytes 772
  52.7 22.4 %all-to-all-start = ((bf16[192,4,1024]{2,0,1:T(8,128)(2,1)}), bf16[192,4,1024]{2,0,1:T(8,128)(2,1)S(1)}, u32[]{:S(2)}, u32[]{:S(2)}) async-start(bf16[192,4,1024]{2,0,1:T(8,128)(2,1)} %bitcast.47), calls=%async_computation | async-start | bytes 3145728 | tf_op jit(solution)/shard_map/all_to_all | solution.py:39
  59.0 24.7 %collective-permute-start.1 = (bf16[768,1024]{1,0:T(8,128)(2,1)}, bf16[768,1024]{1,0:T(8,128)(2,1)}, u32[]{:S(2)}, u32[]{:S(2)}) collective-permute-start(bf16[768,1024]{1,0:T(8,128)(2,1)} %bitcast.3), channel_id=1, source_target_pairs={{4,0},{8,4},{12,8},{16,12},{20,16},{24,20},{28,24},{32,28},{36,32}... | collective-permute-start | bytes 4718600 | tf_op jit(solution)/shard_map/ppermute | solution.py:13
  60.9 22.8 %collective-permute-start = (bf16[768,1024]{1,0:T(8,128)(2,1)}, bf16[768,1024]{1,0:T(8,128)(2,1)}, u32[]{:S(2)}, u32[]{:S(2)}) collective-permute-start(bf16[768,1024]{1,0:T(8,128)(2,1)} %bitcast.3), channel_id=1, source_target_pairs={{0,4},{4,8},{8,12},{12,16},{16,20},{20,24},{24,28},{28,32},{32,36}... | collective-permute-start | bytes 4718600 | tf_op jit(solution)/shard_map/ppermute | solution.py:13
  75.1 1.1 copy-start.1
  76.2 21.5 %all-to-all-start.3 = ((bf16[192,4,1024]{2,0,1:T(8,128)(2,1)}), bf16[192,4,1024]{2,0,1:T(8,128)(2,1)S(1)}, u32[]{:S(2)}, u32[]{:S(2)}) async-start(bf16[192,4,1024]{2,0,1:T(8,128)(2,1)} %bitcast.60), calls=%async_computation.3 | async-start | bytes 3145728 | tf_op jit(solution)/shard_map/all_to_all | solution.py:42
  250.7 11.1 %copy-start = (f32[2304,1024]{1,0:T(8,128)S(1)}, f32[2304,1024]{1,0:T(8,128)}, u32[]{:S(2)}) copy-start(f32[2304,1024]{1,0:T(8,128)} %get-tuple-element.178) | copy-start | bytes 28311556
  257.5 39.7 %collective-permute-start.6 = (f32[768,1024]{1,0:T(8,128)}, f32[768,1024]{1,0:T(8,128)}, u32[]{:S(2)}, u32[]{:S(2)}) collective-permute-start(f32[768,1024]{1,0:T(8,128)} %get-tuple-element.235), channel_id=1, source_target_pairs={{4,0},{8,4},{12,8},{16,12},{20,16},{24,20},{28,24},{32,28},{36,32}... | collective-permute-start | bytes 9437192 | tf_op jit(solution)/shard_map/ppermute | solution.py:13
  259.4 38.9 %collective-permute-start.7 = (f32[768,1024]{1,0:T(8,128)}, f32[768,1024]{1,0:T(8,128)}, u32[]{:S(2)}, u32[]{:S(2)}) collective-permute-start(f32[768,1024]{1,0:T(8,128)} %get-tuple-element.236), channel_id=1, source_target_pairs={{0,4},{4,8},{8,12},{12,16},{16,20},{20,24},{24,28},{28,32},{32,36}... | collective-permute-start | bytes 9437192 | tf_op jit(solution)/shard_map/ppermute | solution.py:13
  265.1 63.1 %collective-permute-start.4 = (f32[768,1024]{1,0:T(8,128)}, f32[768,1024]{1,0:T(8,128)}, u32[]{:S(2)}, u32[]{:S(2)}) collective-permute-start(f32[768,1024]{1,0:T(8,128)} %get-tuple-element.237), channel_id=1, source_target_pairs={{4,0},{8,4},{12,8},{16,12},{20,16},{24,20},{28,24},{32,28},{36,32}... | collective-permute-start | bytes 9437192 | tf_op jit(solution)/shard_map/ppermute | solution.py:13
  268.2 63.8 %collective-permute-start.5 = (f32[768,1024]{1,0:T(8,128)}, f32[768,1024]{1,0:T(8,128)}, u32[]{:S(2)}, u32[]{:S(2)}) collective-permute-start(f32[768,1024]{1,0:T(8,128)} %get-tuple-element.238), channel_id=1, source_target_pairs={{0,4},{4,8},{8,12},{12,16},{16,20},{20,24},{24,28},{28,32},{32,36}... | collective-permute-start | bytes 9437192 | tf_op jit(solution)/shard_map/ppermute | solution.py:13
  293.6 25.5 %all-to-all-start.4 = ((bf16[4,192,1024]{2,1,0:T(8,128)(2,1)}), bf16[4,192,1024]{2,1,0:T(8,128)(2,1)S(1)}, u32[]{:S(2)}, u32[]{:S(2)}) async-start(bf16[4,192,1024]{2,1,0:T(8,128)(2,1)} %bitcast.64), calls=%async_computation.4 | async-start | bytes 3145728 | tf_op jit(solution)/shard_map/all_to_all | solution.py:137
  319.2 25.7 %all-to-all-start.7 = ((bf16[4,192,1024]{2,1,0:T(8,128)(2,1)}), bf16[4,192,1024]{2,1,0:T(8,128)(2,1)}, u32[]{:S(2)}, u32[]{:S(2)}) async-start(bf16[4,192,1024]{2,1,0:T(8,128)(2,1)} %bitcast.65), calls=%async_computation.7 | async-start | bytes 3145728 | tf_op jit(solution)/shard_map/all_to_all | solution.py:140
  344.9 24.8 %all-to-all-start.6 = ((bf16[4,192,1024]{2,1,0:T(8,128)(2,1)}), bf16[4,192,1024]{2,1,0:T(8,128)(2,1)}, u32[]{:S(2)}, u32[]{:S(2)}) async-start(bf16[4,192,1024]{2,1,0:T(8,128)(2,1)} %bitcast.66), calls=%async_computation.6 | async-start | bytes 3145728 | tf_op jit(solution)/shard_map/all_to_all | solution.py:139
where the time goes:
time: 375 us; the launch traced here: 372 us
  matrix products  122 us (33%)
  waiting for transfers between devices  102 us (27%)
  starting transfers between devices  46.2 us (12%)
  other arithmetic  39.6 us (11%)
  local copies, waits for them, and re-layouts  38.6 us (10%)
  blocking collectives  23.3 us (6%)
    dot_general x16, matrix products, contract_first(): lax.dot_general(left, right, (((0,), (0,)), ((), ())), preferred_element_...  43 us
    dot_general x16, matrix products, contract_last(): lax.dot_general(left, right, (((1,), (1,)), ((), ())), preferred_element_...  38.1 us
    all_to_all x1, blocking collectives, on_device(): lax.all_to_all(dq_loc, 'uly', split_axis=0, concat_axis=1, tiled=True)  23.3 us
    dot_general x8, matrix products, query_step(): jnp.dot(weights, value_head, preferred_element_type=jnp.float32)  22.6 us
    all_to_all x1, waiting for transfers between devices, on_device(): lax.all_to_all(values, 'uly', split_axis=1, concat_axis=0, tiled=True)  19.4 us
    ppermute x8, starting transfers between devices, shifted(): return lax.ppermute(value, axis, pairs)  18.2 us
    dot_general x8, matrix products, query_step(): jnp.dot(grad_scores, key_head, preferred_element_type=jnp.float32)  17.8 us
    all_to_all x1, waiting for transfers between devices, on_device(): lax.all_to_all(dk_loc, 'uly', split_axis=0, concat_axis=1, tiled=True)  15.2 us
  transfers between devices with their start and end apart: 15, of which 10 were waited for; matrix products, arithmetic and copies ran while one was open for 9% of the time, Pallas kernels for 0%

commit v1 on v0

--- a/solution.py
+++ b/solution.py
@@ -5,6 +5,29 @@
 
 HEAD_DIM = 128
 masked_score = -1e30
+
+
+def in_blocks(x, dim, size):
+    before, after = (x.shape[:dim], x.shape[dim + 1 :])
+    return jnp.moveaxis(x.reshape(*before, size, -1, *after), dim, 0)
+
+
+def laid_out(parts, dim):
+    dims = list(parts.shape[1:])
+    dims[dim] *= parts.shape[0]
+    return jnp.moveaxis(parts, 0, dim).reshape(dims)
+
+
+def exchange_directly(value, axis, split_dim, concat_dim):
+    size, mine = (lax.axis_size(axis), lax.axis_index(axis))
+    pieces = in_blocks(value, split_dim, size)
+    out = pieces
+    for step in range(1, size):
+        target, source = ((mine + step) % size, (mine - step) % size)
+        sent = lax.dynamic_index_in_dim(pieces, target, 0)
+        other = lax.ppermute(sent, axis, [(i, (i + step) % size) for i in range(size)])
+        out = lax.dynamic_update_slice_in_dim(out, other, source, axis=0)
+    return laid_out(out, concat_dim)
 
 
 def shifted(value, axis, by):
@@ -134,7 +157,7 @@
     dk_loc = key_sum.astype(jnp.bfloat16)
     dv_loc = value_sum.astype(jnp.bfloat16)
     attn_out, d_queries, d_keys, d_values = (
-        lax.all_to_all(out_loc, "uly", split_axis=0, concat_axis=1, tiled=True),
+        exchange_directly(out_loc, "uly", 0, 1),
         lax.all_to_all(dq_loc, "uly", split_axis=0, concat_axis=1, tiled=True),
         lax.all_to_all(dk_loc, "uly", split_axis=0, concat_axis=1, tiled=True),
         lax.all_to_all(dv_loc, "uly", split_axis=0, concat_axis=1, tiled=True),

time: 375 us -> 404 us (1.077)
  waiting for transfers between devices: 102 us -> 144 us
  blocking collectives: 23.3 us -> 0 us
  starting transfers between devices: 46.2 us -> 52.5 us
    ppermute x0 -> x3, waiting for transfers between devices: none -> 44.5 us  [exchange_directly(): lax.ppermute(sent, axis, [(i, (i + step) % size) for i in range(size)])]
    ppermute x8, waiting for transfers between devices: 9.6 us -> 47.2 us  [shifted(): return lax.ppermute(value, axis, pairs)]
    all_to_all x1 -> x0, blocking collectives: 23.3 us -> none  [on_device(): lax.all_to_all(dq_loc, 'uly', split_axis=0, concat_axis=1, tiled=True)]
    all_to_all x1, waiting for transfers between devices: 15.2 us -> 0.01 us  [on_device(): lax.all_to_all(dk_loc, 'uly', split_axis=0, concat_axis=1, tiled=True)]
    all_to_all x1, waiting for transfers between devices: 15.1 us -> 0.01 us  [on_device(): lax.all_to_all(dq_loc, 'uly', split_axis=0, concat_axis=1, tiled=True)]
    all_to_all x1, waiting for transfers between devices: 7.04 us -> 0.01 us  [on_device(): lax.all_to_all(dv_loc, 'uly', split_axis=0, concat_axis=1, tiled=True)]
    all_to_all x1, waiting for transfers between devices: 19.4 us -> 13 us  [on_device(): lax.all_to_all(values, 'uly', split_axis=1, concat_axis=0, tiled=True)]
    all_to_all x1, waiting for transfers between devices: 14.2 us -> 19.4 us  [on_device(): lax.all_to_all(keys, 'uly', split_axis=1, concat_axis=0, tiled=True)]
  transfers between devices with their start and end apart: 15 -> 18, of which waited for: 10 -> 10; matrix products, arithmetic and copies ran while one was open for 9% -> 9% of each run, Pallas kernels for 0% -> 0%
where the time goes in v1:
time: 404 us; the launch traced here: 401 us
  waiting for transfers between devices  144 us (36%)
  matrix products  122 us (30%)
  starting transfers between devices  52.5 us (13%)
  local copies, waits for them, and re-layouts  41.4 us (10%)
  other arithmetic  39.6 us (10%)
    ppermute x8, waiting for transfers between devices, shifted(): return lax.ppermute(value, axis, pairs)  47.2 us
    ppermute x3, waiting for transfers between devices, exchange_directly(): lax.ppermute(sent, axis, [(i, (i + step) % size) for i in range(size)])  44.5 us
    dot_general x16, matrix products, contract_first(): lax.dot_general(left, right, (((0,), (0,)), ((), ())), preferred_element_...  43.1 us
    dot_general x16, matrix products, contract_last(): lax.dot_general(left, right, (((1,), (1,)), ((), ())), preferred_element_...  38.1 us
    dot_general x8, matrix products, query_step(): jnp.dot(grad_scores, key_head, preferred_element_type=jnp.float32)  22.6 us
    ppermute x8, starting transfers between devices, shifted(): return lax.ppermute(value, axis, pairs)  21.2 us
    all_to_all x1, waiting for transfers between devices, on_device(): lax.all_to_all(keys, 'uly', split_axis=1, concat_axis=0, tiled=True)  19.4 us
    dot_general x8, matrix products, query_step(): jnp.dot(weights, value_head, preferred_element_type=jnp.float32)  17.9 us
  transfers between devices with their start and end apart: 18, of which 10 were waited for; matrix products, arithmetic and copies ran while one was open for 9% of the time, Pallas kernels for 0%

profile of v1, /device:TPU:88, one launch (start us, length us, event | category | flops | bytes accessed | tf_op | source)
XLA Modules:
  0.0 400.9 jit_solution(14824610078051956199)
XLA Ops:
  0.6 2.8 copy.54
  3.5 4.3 %all-to-all-start.1 = ((bf16[192,4,1024]{2,0,1:T(8,128)(2,1)}), bf16[192,4,1024]{2,0,1:T(8,128)(2,1)S(1)}, u32[]{:S(2)}, u32[]{:S(2)}) async-start(bf16[192,4,1024]{2,0,1:T(8,128)(2,1)} %bitcast.46), calls=%async_computation.1 | async-start | bytes 3145728 | tf_op jit(solution)/shard_map/all_to_all | solution.py:63
  9.1 19.4 %all-to-all-done.1 = bf16[192,4,1024]{2,0,1:T(8,128)(2,1)S(1)} async-done(((bf16[192,4,1024]{2,0,1:T(8,128)(2,1)}), bf16[192,4,1024]{2,0,1:T(8,128)(2,1)S(1)}, u32[]{:S(2)}, u32[]{:S(2)}) %all-to-all-start.1) | async-done | bytes 1572896 | tf_op jit(solution)/shard_map/all_to_all | solution.py:63
  28.5 4.4 %all-to-all-start.2 = ((bf16[192,4,1024]{2,0,1:T(8,128)(2,1)}), bf16[192,4,1024]{2,0,1:T(8,128)(2,1)}, u32[]{:S(2)}, u32[]{:S(2)}) async-start(bf16[192,4,1024]{2,0,1:T(8,128)(2,1)} %bitcast.45), calls=%async_computation.2 | async-start | bytes 3145728 | tf_op jit(solution)/shard_map/all_to_all | solution.py:64
  34.8 3.6 collective-permute-start.1
  39.7 13.0 %all-to-all-done.2 = bf16[192,4,1024]{2,0,1:T(8,128)(2,1)} async-done(((bf16[192,4,1024]{2,0,1:T(8,128)(2,1)}), bf16[192,4,1024]{2,0,1:T(8,128)(2,1)}, u32[]{:S(2)}, u32[]{:S(2)}) %all-to-all-start.2) | async-done | bytes 1572896 | tf_op jit(solution)/shard_map/all_to_all | solution.py:64
  52.7 3.7 all-to-all-start
  56.4 2.7 copy.52
  61.0 3.6 collective-permute-start.3
  65.0 10.2 %all-to-all-done = bf16[192,4,1024]{2,0,1:T(8,128)(2,1)S(1)} async-done(((bf16[192,4,1024]{2,0,1:T(8,128)(2,1)}), bf16[192,4,1024]{2,0,1:T(8,128)(2,1)S(1)}, u32[]{:S(2)}, u32[]{:S(2)}) %all-to-all-start) | async-done | bytes 1572896 | tf_op jit(solution)/shard_map/all_to_all | solution.py:62
  76.4 3.6 all-to-all-start.3
  80.0 3.8 pad_maximum_fusion
  83.8 4.0 pad_maximum_fusion.1
  87.8 10.1 %all-to-all-done.3 = bf16[192,4,1024]{2,0,1:T(8,128)(2,1)S(1)} async-done(((bf16[192,4,1024]{2,0,1:T(8,128)(2,1)}), bf16[192,4,1024]{2,0,1:T(8,128)(2,1)S(1)}, u32[]{:S(2)}, u32[]{:S(2)}) %all-to-all-start.3) | async-done | bytes 1572896 | tf_op jit(solution)/shard_map/all_to_all | solution.py:65
  97.9 4.8 %broadcast.65 = f32[2304,1024]{1,0:T(8,128)} broadcast(f32[]{:T(128)} %constant.114.clone.1), dimensions={} | broadcast | bytes 9437188 | tf_op jit(solution)/shard_map/broadcast.9
  102.7 4.9 %broadcast.65.clone = f32[2304,1024]{1,0:T(8,128)} broadcast(f32[]{:T(128)} %constant.114.clone.1), dimensions={} | broadcast | bytes 9437188 | tf_op jit(solution)/shard_map/broadcast.9
  109.1 141.9 %while.20 = (s32[]{:T(128)}, bf16[768,1024]{1,0:T(8,128)(2,1)S(1)}, bf16[768,1024]{1,0:T(8,128)(2,1)}, f32[2304,1024]{1,0:T(8,128)}, f32[2304,1024]{1,0:T(8,128)...) while((s32[]{:T(128)}, bf16[768,1024]{1,0:T(8,128)(2,1)S(1)}, ...), condition=%wide.region_8.9_spmd.clone, body=%wide.region_4.8_spmd.clone.sunk | while | flops 2740124160 | bytes 52541632 | solution.py:143
  109.1 2.6 fusion.47
  118.6 3.2 fusion.49
  124.0 2.8 fusion.48
  126.8 2.6 fusion.47
  131.7 2.2 constant_dynamic-update-slice_fusion.5
  136.4 3.2 fusion.49
  141.7 2.8 fusion.48
  144.5 2.6 fusion.47
  149.4 2.2 constant_dynamic-update-slice_fusion.5
  154.1 3.2 fusion.49
  159.5 2.8 fusion.48
  162.3 2.6 fusion.47
  167.2 2.2 constant_dynamic-update-slice_fusion.5
  171.8 3.2 fusion.49
  177.2 2.8 fusion.48
  180.1 2.6 fusion.47
  185.0 2.2 constant_dynamic-update-slice_fusion.5
  189.6 3.2 fusion.49
  192.8 2.3 convolution_dynamic-update-slice_fusion.2
  195.1 2.8 fusion.48
  197.9 2.6 fusion.47
  207.4 3.2 fusion.49
  212.8 2.8 fusion.48
  215.6 2.6 fusion.47
  220.5 2.2 constant_dynamic-update-slice_fusion.5
  225.2 3.1 fusion.49
  230.5 2.8 fusion.48
  233.3 2.6 fusion.47
  238.3 2.2 constant_dynamic-update-slice_fusion.5
  242.9 3.1 fusion.49
  248.2 2.8 fusion.48
  251.1 6.8 %fusion.20 = (f32[768,1024]{1,0:T(8,128)}, f32[768,1024]{1,0:T(8,128)}) fusion(f32[2304,1024]{1,0:T(8,128)} %get-tuple-element.179), kind=kLoop, calls=%fused_computation.56 | loop fusion | bytes 12582912 | tf_op jit(solution)/shard_map/slice | solution.py:151
  259.7 3.6 collective-permute-start.9
  263.4 3.3 fusion.21
  268.6 2.6 collective-permute-start.8
  271.2 3.6 all-to-all-start.4
  274.8 21.9 %collective-permute-done.10 = f32[768,1024]{1,0:T(8,128)} collective-permute-done((f32[768,1024]{1,0:T(8,128)}, f32[768,1024]{1,0:T(8,128)}, u32[]{:S(2)}, u32[]{:S(2)}) %collective-permute-start.10) | collective-permute-done | bytes 3145760 | tf_op jit(solution)/shard_map/ppermute | solution.py:36
  298.5 5.8 %add_convert_fusion = bf16[768,1024]{1,0:T(8,128)(2,1)} fusion(f32[768,1024]{1,0:T(8,128)} %collective-permute-done.10, f32[768,1024]{1,0:T(8,128)} %collective-permute-done.9, f32[2304,1024]{1,0:T(8,128)} %get-tuple-element.179), kind=kLoop, calls=%fused_computation.31 | loop fusion | flops 2359296 | bytes 11010048 | tf_op jit(solution)/shard_map/convert_element_type | solution.py:158
  304.3 4.4 %all-to-all-start.6 = ((bf16[4,192,1024]{2,1,0:T(8,128)(2,1)}), bf16[4,192,1024]{2,1,0:T(8,128)(2,1)}, u32[]{:S(2)}, u32[]{:S(2)}) async-start(bf16[4,192,1024]{2,1,0:T(8,128)(2,1)} %bitcast.67), calls=%async_computation.6 | async-start | bytes 3145728 | tf_op jit(solution)/shard_map/all_to_all | solution.py:163
  308.7 23.5 %collective-permute-done.7 = f32[768,1024]{1,0:T(8,128)} collective-permute-done((f32[768,1024]{1,0:T(8,128)}, f32[768,1024]{1,0:T(8,128)}, u32[]{:S(2)}, u32[]{:S(2)}) %collective-permute-start.7) | collective-permute-done | bytes 3145760 | tf_op jit(solution)/shard_map/ppermute | solution.py:36
  332.2 5.8 %add_convert_fusion.1 = bf16[768,1024]{1,0:T(8,128)(2,1)} fusion(f32[768,1024]{1,0:T(8,128)} %collective-permute-done.8, f32[768,1024]{1,0:T(8,128)} %collective-permute-done.7, f32[2304,1024]{1,0:T(8,128)} %get-tuple-element.178), kind=kLoop, calls=%fused_computation.32 | loop fusion | flops 2359296 | bytes 11010048 | tf_op jit(solution)/shard_map/convert_element_type | solution.py:157
  338.0 4.4 %all-to-all-start.5 = ((bf16[4,192,1024]{2,1,0:T(8,128)(2,1)}), bf16[4,192,1024]{2,1,0:T(8,128)(2,1)}, u32[]{:S(2)}, u32[]{:S(2)}) async-start(bf16[4,192,1024]{2,1,0:T(8,128)(2,1)} %bitcast.66), calls=%async_computation.5 | async-start | bytes 3145728 | tf_op jit(solution)/shard_map/all_to_all | solution.py:162
  345.1 26.5 %collective-permute-done.4 = bf16[1,192,1024]{2,1,0:T(8,128)(2,1)S(1)} collective-permute-done((bf16[1,192,1024]{2,1,0:T(8,128)(2,1)}, bf16[1,192,1024]{2,1,0:T(8,128)(2,1)S(1)}, u32[]{:S(2)}, u32[]{:S(2)}) %collective-permute-start.4) | collective-permute-done | bytes 393248 | tf_op jit(solution)/shard_map/ppermute | solution.py:28
  373.8 12.4 %collective-permute-done.5 = bf16[1,192,1024]{2,1,0:T(8,128)(2,1)} collective-permute-done((bf16[1,192,1024]{2,1,0:T(8,128)(2,1)}, bf16[1,192,1024]{2,1,0:T(8,128)(2,1)}, u32[]{:S(2)}, u32[]{:S(2)}) %collective-permute-start.5) | collective-permute-done | bytes 393248 | tf_op jit(solution)/shard_map/ppermute | solution.py:28
  387.2 5.6 %collective-permute-done.6 = bf16[1,192,1024]{2,1,0:T(8,128)(2,1)S(1)} collective-permute-done((bf16[1,192,1024]{2,1,0:T(8,128)(2,1)}, bf16[1,192,1024]{2,1,0:T(8,128)(2,1)S(1)}, u32[]{:S(2)}, u32[]{:S(2)}) %collective-permute-start.6) | collective-permute-done | bytes 393248 | tf_op jit(solution)/shard_map/ppermute | solution.py:28
  395.4 2.7 copy.47
  398.1 2.7 copy.46
  (93 shorter events, 80.8 us)
Async XLA Ops:
  0.6 7.1 %copy-start.2 = (bf16[192,4096]{1,0:T(8,128)(2,1)S(1)}, bf16[192,4096]{1,0:T(8,128)(2,1)}, u32[]{:S(2)}) copy-start(bf16[192,4096]{1,0:T(8,128)(2,1)} %param.9) | copy-start | bytes 4718596
  3.5 25.0 %all-to-all-start.1 = ((bf16[192,4,1024]{2,0,1:T(8,128)(2,1)}), bf16[192,4,1024]{2,0,1:T(8,128)(2,1)S(1)}, u32[]{:S(2)}, u32[]{:S(2)}) async-start(bf16[192,4,1024]{2,0,1:T(8,128)(2,1)} %bitcast.46), calls=%async_computation.1 | async-start | bytes 3145728 | tf_op jit(solution)/shard_map/all_to_all | solution.py:63
  9.1 29.4 %copy-start.3 = (bf16[192,4096]{1,0:T(8,128)(2,1)S(1)}, bf16[192,4096]{1,0:T(8,128)(2,1)}, u32[]{:S(2)}) copy-start(bf16[192,4096]{1,0:T(8,128)(2,1)} %param.7) | copy-start | bytes 4718596
  28.5 24.2 %all-to-all-start.2 = ((bf16[192,4,1024]{2,0,1:T(8,128)(2,1)}), bf16[192,4,1024]{2,0,1:T(8,128)(2,1)}, u32[]{:S(2)}, u32[]{:S(2)}) async-start(bf16[192,4,1024]{2,0,1:T(8,128)(2,1)} %bitcast.45), calls=%async_computation.2 | async-start | bytes 3145728 | tf_op jit(solution)/shard_map/all_to_all | solution.py:64
  32.8 47.2 %collective-permute-start = (bf16[768,1024]{1,0:T(8,128)(2,1)S(1)}, bf16[768,1024]{1,0:T(8,128)(2,1)}, u32[]{:S(2)}, u32[]{:S(2)}) collective-permute-start(bf16[768,1024]{1,0:T(8,128)(2,1)S(1)} %bitcast.61), channel_id=1, source_target_pairs={{0,4},{4,8},{8,12},{12,16},{16,20},{20,24},{24,28},{28,32},{32,36}... | collective-permute-start | bytes 4718600 | tf_op jit(solution)/shard_map/ppermute | solution.py:36
  34.8 45.2 %collective-permute-start.1 = (bf16[768,1024]{1,0:T(8,128)(2,1)S(1)}, bf16[768,1024]{1,0:T(8,128)(2,1)}, u32[]{:S(2)}, u32[]{:S(2)}) collective-permute-start(bf16[768,1024]{1,0:T(8,128)(2,1)S(1)} %bitcast.62), channel_id=1, source_target_pairs={{4,0},{8,4},{12,8},{16,12},{20,16},{24,20},{28,24},{32,28},{36,32}... | collective-permute-start | bytes 4718600 | tf_op jit(solution)/shard_map/ppermute | solution.py:36
  52.7 12.0 %copy-start.4 = (s32[64]{0:T(128)S(1)}, s32[64]{0:T(128)}, u32[]{:S(2)}) copy-start(s32[64]{0:T(128)} %param.11) | copy-start | bytes 772
  52.7 22.5 %all-to-all-start = ((bf16[192,4,1024]{2,0,1:T(8,128)(2,1)}), bf16[192,4,1024]{2,0,1:T(8,128)(2,1)S(1)}, u32[]{:S(2)}, u32[]{:S(2)}) async-start(bf16[192,4,1024]{2,0,1:T(8,128)(2,1)} %bitcast.47), calls=%async_computation | async-start | bytes 3145728 | tf_op jit(solution)/shard_map/all_to_all | solution.py:62
  59.1 24.7 %collective-permute-start.2 = (bf16[768,1024]{1,0:T(8,128)(2,1)}, bf16[768,1024]{1,0:T(8,128)(2,1)}, u32[]{:S(2)}, u32[]{:S(2)}) collective-permute-start(bf16[768,1024]{1,0:T(8,128)(2,1)} %bitcast.6), channel_id=1, source_target_pairs={{0,4},{4,8},{8,12},{12,16},{16,20},{20,24},{24,28},{28,32},{32,36}... | collective-permute-start | bytes 4718600 | tf_op jit(solution)/shard_map/ppermute | solution.py:36
  61.0 22.8 %collective-permute-start.3 = (bf16[768,1024]{1,0:T(8,128)(2,1)}, bf16[768,1024]{1,0:T(8,128)(2,1)}, u32[]{:S(2)}, u32[]{:S(2)}) collective-permute-start(bf16[768,1024]{1,0:T(8,128)(2,1)} %bitcast.6), channel_id=1, source_target_pairs={{4,0},{8,4},{12,8},{16,12},{20,16},{24,20},{28,24},{32,28},{36,32}... | collective-permute-start | bytes 4718600 | tf_op jit(solution)/shard_map/ppermute | solution.py:36
  75.2 1.1 copy-start.1
  76.4 21.5 %all-to-all-start.3 = ((bf16[192,4,1024]{2,0,1:T(8,128)(2,1)}), bf16[192,4,1024]{2,0,1:T(8,128)(2,1)S(1)}, u32[]{:S(2)}, u32[]{:S(2)}) async-start(bf16[192,4,1024]{2,0,1:T(8,128)(2,1)} %bitcast.64), calls=%async_computation.3 | async-start | bytes 3145728 | tf_op jit(solution)/shard_map/all_to_all | solution.py:65
  251.1 12.3 %copy-start = (f32[2304,1024]{1,0:T(8,128)S(1)}, f32[2304,1024]{1,0:T(8,128)}, u32[]{:S(2)}) copy-start(f32[2304,1024]{1,0:T(8,128)} %get-tuple-element.178) | copy-start | bytes 28311556
  257.8 38.9 %collective-permute-start.10 = (f32[768,1024]{1,0:T(8,128)}, f32[768,1024]{1,0:T(8,128)}, u32[]{:S(2)}, u32[]{:S(2)}) collective-permute-start(f32[768,1024]{1,0:T(8,128)} %get-tuple-element.236), channel_id=1, source_target_pairs={{0,4},{4,8},{8,12},{12,16},{16,20},{20,24},{24,28},{28,32},{32,36}... | collective-permute-start | bytes 9437192 | tf_op jit(solution)/shard_map/ppermute | solution.py:36
  259.7 38.7 %collective-permute-start.9 = (f32[768,1024]{1,0:T(8,128)}, f32[768,1024]{1,0:T(8,128)}, u32[]{:S(2)}, u32[]{:S(2)}) collective-permute-start(f32[768,1024]{1,0:T(8,128)} %get-tuple-element.235), channel_id=1, source_target_pairs={{4,0},{8,4},{12,8},{16,12},{20,16},{24,20},{28,24},{32,28},{36,32}... | collective-permute-start | bytes 9437192 | tf_op jit(solution)/shard_map/ppermute | solution.py:36
  266.7 65.5 %collective-permute-start.7 = (f32[768,1024]{1,0:T(8,128)}, f32[768,1024]{1,0:T(8,128)}, u32[]{:S(2)}, u32[]{:S(2)}) collective-permute-start(f32[768,1024]{1,0:T(8,128)} %get-tuple-element.237), channel_id=1, source_target_pairs={{4,0},{8,4},{12,8},{16,12},{20,16},{24,20},{28,24},{32,28},{36,32}... | collective-permute-start | bytes 9437192 | tf_op jit(solution)/shard_map/ppermute | solution.py:36
  268.6 63.6 %collective-permute-start.8 = (f32[768,1024]{1,0:T(8,128)}, f32[768,1024]{1,0:T(8,128)}, u32[]{:S(2)}, u32[]{:S(2)}) collective-permute-start(f32[768,1024]{1,0:T(8,128)} %get-tuple-element.238), channel_id=1, source_target_pairs={{0,4},{4,8},{8,12},{12,16},{16,20},{20,24},{24,28},{28,32},{32,36}... | collective-permute-start | bytes 9437192 | tf_op jit(solution)/shard_map/ppermute | solution.py:36
  271.2 33.1 %all-to-all-start.4 = ((bf16[4,192,1024]{2,1,0:T(8,128)(2,1)}), bf16[4,192,1024]{2,1,0:T(8,128)(2,1)S(1)}, u32[]{:S(2)}, u32[]{:S(2)}) async-start(bf16[4,192,1024]{2,1,0:T(8,128)(2,1)} %bitcast.65), calls=%async_computation.4 | async-start | bytes 3145728 | tf_op jit(solution)/shard_map/all_to_all | solution.py:161
  304.3 33.7 %all-to-all-start.6 = ((bf16[4,192,1024]{2,1,0:T(8,128)(2,1)}), bf16[4,192,1024]{2,1,0:T(8,128)(2,1)}, u32[]{:S(2)}, u32[]{:S(2)}) async-start(bf16[4,192,1024]{2,1,0:T(8,128)(2,1)} %bitcast.67), calls=%async_computation.6 | async-start | bytes 3145728 | tf_op jit(solution)/shard_map/all_to_all | solution.py:163
  338.0 60.2 %all-to-all-start.5 = ((bf16[4,192,1024]{2,1,0:T(8,128)(2,1)}), bf16[4,192,1024]{2,1,0:T(8,128)(2,1)}, u32[]{:S(2)}, u32[]{:S(2)}) async-start(bf16[4,192,1024]{2,1,0:T(8,128)(2,1)} %bitcast.66), calls=%async_computation.5 | async-start | bytes 3145728 | tf_op jit(solution)/shard_map/all_to_all | solution.py:162
  343.1 28.5 %collective-permute-start.4 = (bf16[1,192,1024]{2,1,0:T(8,128)(2,1)}, bf16[1,192,1024]{2,1,0:T(8,128)(2,1)S(1)}, u32[]{:S(2)}, u32[]{:S(2)}) collective-permute-start(bf16[1,192,1024]{2,1,0:T(8,128)(2,1)} %constant_dynamic-slice_fusion.2), channel_id=1, source_target_pairs={{0,1},{1,2},{2,3},{3,0},{4,5},{5,6},{6,7},{7,4},{8,9},{9,10},{10,1... | collective-permute-start | bytes 1179656 | tf_op jit(solution)/shard_map/ppermute | solution.py:28
  372.6 13.6 %collective-permute-start.5 = (bf16[1,192,1024]{2,1,0:T(8,128)(2,1)}, bf16[1,192,1024]{2,1,0:T(8,128)(2,1)}, u32[]{:S(2)}, u32[]{:S(2)}) collective-permute-start(bf16[1,192,1024]{2,1,0:T(8,128)(2,1)} %get-tuple-element.240), channel_id=1, source_target_pairs={{0,2},{1,3},{2,0},{3,1},{4,6},{5,7},{6,4},{7,5},{8,10},{9,11},{10,... | collective-permute-start | bytes 1179656 | tf_op jit(solution)/shard_map/ppermute | solution.py:28
  373.4 19.3 %collective-permute-start.6 = (bf16[1,192,1024]{2,1,0:T(8,128)(2,1)}, bf16[1,192,1024]{2,1,0:T(8,128)(2,1)S(1)}, u32[]{:S(2)}, u32[]{:S(2)}) collective-permute-start(bf16[1,192,1024]{2,1,0:T(8,128)(2,1)} %get-tuple-element.239), channel_id=1, source_target_pairs={{0,3},{1,0},{2,1},{3,2},{4,7},{5,4},{6,5},{7,6},{8,11},{9,8},{10,9... | collective-permute-start | bytes 1179656 | tf_op jit(solution)/shard_map/ppermute | solution.py:28
